TPU v7x, 32 devices: a whole 2x2x4 slice. The times are simulated.
32 devices in a mesh: tm: 8 (over z, core), neuron: 4 (over y, x).
Axes of the slice: x: 2, y: 2, z: 4, core: 2. Of those that a mesh axis runs over, the one named last changes fastest.
Arguments:
- observations: bfloat16 [1024, 12800], P('tm', 'neuron'), may hold values from -6 to 6
- loadings: bfloat16 [512, 12800], P(None, 'neuron'), may hold values from -0.01953125 to 0.01953125
- region_mask: int32 [4, 100], P(None, 'neuron'), may hold values 0 or 1
- precision: float32 [12800], P('neuron'), may hold values from 0.5 to 8
- decay_rate: bfloat16 [1024, 512], P('tm'), may hold values from 9.667969e-05 to 0.42
- smoothing_lag: float32 [512], replicated, may hold values from 0.5 to 1.25
Outputs:
- loading_grad: bfloat16 [512, 12800], P('tm', 'neuron')
All inputs are finite; a program needn't handle non-finite values. No bound on the sum of `region_mask` on one device may be relied on, other than what follows from the above.
Results may differ from a plain program's by a relative error of at most 0.0064.
Values may be sent and summed in bfloat16 or wider, within the bound.
A program may use at most 128 MiB of HBM per device.

v0:
```python
import math

import jax
import jax.numpy as jnp
from jax import lax
from jax.sharding import PartitionSpec as P

LATENT_GROUP = 128
REGION = 128


def prefix(part, axis, combine, identity, reverse):
    count = lax.axis_size(axis)
    place = lax.axis_index(axis)
    ahead = count - 1 - place if reverse else place
    gathered = jax.tree.map(lambda a: lax.all_gather(a, axis), part)
    state = jax.tree.map(lambda a, e: jnp.zeros_like(a) + jnp.asarray(e, a.dtype), part, identity)

    def one(lap, state):
        source = count - 1 - lap if reverse else lap
        return combine(
            state, jax.tree.map(lambda a: lax.dynamic_index_in_dim(a, source, 0, False), gathered)
        )

    return lax.fori_loop(0, ahead, one, state)


def combine(earlier, latter):
    return (earlier[0] * latter[0], latter[0] * earlier[1] + latter[1])


def expand_mask(region_mask):
    groups, regions = region_mask.shape
    widened = jnp.broadcast_to(
        region_mask[:, None, :, None], (groups, LATENT_GROUP, regions, REGION)
    )
    return widened.reshape(groups * LATENT_GROUP, regions * REGION).astype(jnp.bfloat16)


def per_device(observations, loadings, region_mask, precision, decay_rate, smoothing_lag):
    mask_full = expand_mask(region_mask)
    effective = loadings * mask_full
    weighted = (effective.astype(jnp.float32) * precision[None, :]).astype(jnp.bfloat16)
    frames = observations.shape[0]
    latents = loadings.shape[0]
    total_frames = frames * lax.axis_size("tm")
    share_rows = frames // lax.axis_size("neuron")
    picked = observations
    driving = lax.psum_scatter(
        lax.dot_general(
            picked, weighted, (((1,), (1,)), ((), ())), preferred_element_type=jnp.float32
        ),
        "neuron",
        scatter_dimension=0,
        tiled=True,
    )
    rate_rows = lax.dynamic_slice_in_dim(
        decay_rate, lax.axis_index("neuron") * share_rows, share_rows, 0
    ).astype(jnp.float32)
    decays = jnp.exp(-rate_rows)
    innovation = jnp.sqrt(-jnp.expm1(-2.0 * rate_rows))
    forward_mult, forward_add = lax.associative_scan(
        combine, (decays, innovation * driving), axis=0
    )
    identity = (jnp.ones((latents,), jnp.float32), jnp.zeros((latents,), jnp.float32))
    block_total = (forward_mult[-1], forward_add[-1])
    entering = prefix(block_total, ("tm", "neuron"), combine, identity, False)
    filtered = forward_mult * entering[1][None, :] + forward_add
    retained = jnp.exp(-rate_rows * smoothing_lag[None, :])
    backward_mult, backward_add = lax.associative_scan(
        combine, (retained[::-1], ((1.0 - retained) * filtered)[::-1]), axis=0
    )
    block_back = (backward_mult[-1], backward_add[-1])
    following = prefix(block_back, ("tm", "neuron"), combine, identity, True)
    smoothed = (backward_mult * following[1][None, :] + backward_add)[::-1].astype(jnp.bfloat16)
    smoothed = lax.all_gather(smoothed, "neuron", axis=0, tiled=True)
    rebuilt = jnp.dot(smoothed, effective, preferred_element_type=jnp.float32)
    residual = ((observations.astype(jnp.float32) - rebuilt) * precision[None, :]).astype(
        jnp.bfloat16
    )
    grad_scale = 1.0 / math.sqrt(total_frames)
    owned_rows = latents // lax.axis_size("tm")
    mask_rows = lax.dynamic_slice_in_dim(
        mask_full, lax.axis_index("tm") * owned_rows, owned_rows, 0
    ).astype(jnp.float32)
    picked = smoothed
    summed = lax.psum_scatter(
        lax.dot_general(
            picked, residual, (((0,), (0,)), ((), ())), preferred_element_type=jnp.float32
        ),
        "tm",
        scatter_dimension=0,
        tiled=True,
    )
    return (summed * grad_scale * mask_rows).astype(jnp.bfloat16)


def solution(mesh):
    return jax.shard_map(
        per_device,
        mesh=mesh,
        in_specs=(
            P("tm", "neuron"),
            P(None, "neuron"),
            P(None, "neuron"),
            P("neuron"),
            P("tm", None),
            P(),
        ),
        out_specs=P("tm", "neuron"),
        check_vma=False,
    )
```

profile of v0, /device:TPU:0, one launch (start us, length us, event | category | flops | bytes accessed | tf_op | source)
XLA Modules:
  0.0 466.0 jit_solution(7229522176800409977)
XLA Ops:
  7.3 5.7 %copy.101 = bf16[512,3200]{0,1:T(8,128)(2,1)} copy(bf16[512,3200]{1,0:T(8,128)(2,1)} %param.11) | data formatting | bytes 6553600 | tf_op args[1]
  13.0 0.9 broadcast_in_dim.5
  13.9 1.0 copy-done
  14.9 3.2 fusion.5
  18.2 0.8 copy.104
  19.1 26.9 %reduce-scatter.7.cloned.1.call-done = f32[32,512]{1,0:T(8,128)} async-done(((f32[128,512]{1,0:T(8,128)}), f32[32,512]{1,0:T(8,128)}) %reduce-scatter.7.cloned.1.call-update) | async-done | bytes 65552 | tf_op jit(solution)/shard_map/reduce_scatter | solution.py:49
  45.9 0.9 fusion.7
  49.8 0.8 pad.153
  50.6 66.9 %all-gather.2 = f32[32,1,512]{2,1,0:T(1,128)S(1)} all-gather(f32[1,1,512]{2,1,0:T(1,128)S(1)} %add_bitcast_fusion.1), channel_id=1, replica_groups=mesh['tm'=8,'neuron'=4] {'tm','neuron'}, dimensions={0}, use_global_device_ids=true | all-gather | bytes 67584 | tf_op jit(solution)/shard_map/all_gather | solution.py:16
  118.0 0.8 pad_maximum_fusion.1
  118.8 0.8 pad.143
  119.7 63.7 %all-gather.1 = f32[32,1,512]{2,1,0:T(1,128)S(1)} all-gather(f32[1,1,512]{2,1,0:T(1,128)S(1)} %add_bitcast_fusion.2), channel_id=1, replica_groups=mesh['tm'=8,'neuron'=4] {'tm','neuron'}, dimensions={0}, use_global_device_ids=true | all-gather | bytes 67584 | tf_op jit(solution)/shard_map/all_gather | solution.py:16
  184.0 0.9 fusion.9
  185.1 1.2 slice.314
  186.6 0.8 fusion.32
  191.7 88.4 %all-gather.3 = f32[32,1,512]{2,1,0:T(1,128)S(1)} all-gather(f32[1,1,512]{2,1,0:T(1,128)S(1)} %add_bitcast_fusion), channel_id=1, replica_groups=mesh['tm'=8,'neuron'=4] {'tm','neuron'}, dimensions={0}, use_global_device_ids=true | all-gather | bytes 67584 | tf_op jit(solution)/shard_map/all_gather | solution.py:16
  280.8 0.8 pad.133
  281.6 63.7 %all-gather = f32[32,1,512]{2,1,0:T(1,128)S(1)} all-gather(f32[1,1,512]{2,1,0:T(1,128)S(1)} %add_bitcast_fusion.3), channel_id=1, replica_groups=mesh['tm'=8,'neuron'=4] {'tm','neuron'}, dimensions={0}, use_global_device_ids=true | all-gather | bytes 67584 | tf_op jit(solution)/shard_map/all_gather | solution.py:16
  345.9 24.0 %while.27 = (s32[]{:T(128)}, f32[512]{0:T(512)S(1)}, s32[]{:T(128)}, f32[32,512]{1,0:T(8,128)}, f32[32,512]{1,0:T(8,128)}, /*index=5*/s32[]{:T(128)}, s32[]{:T(128)}, s32[]{:T(128)}, s32[]{:T(128)}) while((s32[]{:T(128)}, f32[512]{0:T(512)S(1)}, s32[]{:T(128)}, f32[32,512]{1,0:T(8,128)}, f32[32,512]{1,0:T(8,128)}, /*index=5*/s32[]{:T(128)}, ...), condition=%wide.region_4.5_spmd, body=%wide.region_3.4_spmd.sunk | while | flops 1030 | bytes 16535 | solution.py:25
  346.6 0.7 constant_dynamic-slice_fusion.8
  347.4 0.7 constant_dynamic-slice_fusion.8
  348.2 0.7 constant_dynamic-slice_fusion.8
  349.0 0.7 constant_dynamic-slice_fusion.8
  349.7 0.7 constant_dynamic-slice_fusion.8
  350.5 0.7 constant_dynamic-slice_fusion.8
  351.3 0.7 constant_dynamic-slice_fusion.8
  352.1 0.7 constant_dynamic-slice_fusion.8
  352.8 0.7 constant_dynamic-slice_fusion.8
  353.6 0.7 constant_dynamic-slice_fusion.8
  354.4 0.7 constant_dynamic-slice_fusion.8
  355.2 0.7 constant_dynamic-slice_fusion.8
  355.9 0.7 constant_dynamic-slice_fusion.8
  356.7 0.7 constant_dynamic-slice_fusion.8
  357.5 0.7 constant_dynamic-slice_fusion.8
  358.3 0.7 constant_dynamic-slice_fusion.8
  359.0 0.7 constant_dynamic-slice_fusion.8
  359.8 0.7 constant_dynamic-slice_fusion.8
  360.6 0.7 constant_dynamic-slice_fusion.8
  361.4 0.7 constant_dynamic-slice_fusion.8
  362.1 0.7 constant_dynamic-slice_fusion.8
  368.3 0.7 constant_dynamic-slice_fusion.8
  370.5 1.4 rev.2
  372.0 8.5 %all_gather.19 = bf16[128,512]{1,0:T(8,128)(2,1)S(1)} all-gather(bf16[32,512]{1,0:T(8,128)(2,1)S(1)} %rev.2), channel_id=1, replica_groups=mesh['tm'=8,'neuron'=4] {'neuron'}, dimensions={0}, use_global_device_ids=true | all-gather | bytes 163840 | tf_op jit(solution)/shard_map/all_gather | solution.py:76
  380.4 7.0 %fusion.4 = f32[512,3200]{1,0:T(8,128)} fusion(bf16[128,512]{1,0:T(8,128)(2,1)S(1)} %all_gather.19, bf16[128,3200]{1,0:T(8,128)(2,1)} %param.10, f32[3200]{0:T(1024)} %param.13, bf16[512,3200]{0,1:T(8,128)(2,1)} %copy.101, bf16[400,8,4,128]{3,2,1,0:T(4,128)(2,1)S(1)} %bitcast.53), kind=kOutput, calls=%fused_computation.13 | convolution fusion | flops 842137600 | bytes 14070272 | tf_op jit(solution)/shard_map/dot_general | solution.py:88
  387.5 2.3 copy.124
  389.8 1.6 constant_dynamic-slice_fusion.4
  391.7 65.4 %reduce-scatter.5.cloned.1.call-done = f32[64,3200]{1,0:T(8,128)} async-done(((f32[512,3200]{1,0:T(8,128)}), f32[64,3200]{1,0:T(8,128)}) %reduce-scatter.5.cloned.1.call-update) | async-done | bytes 819216 | tf_op jit(solution)/shard_map/reduce_scatter | solution.py:87
  457.1 2.0 multiply_convert_fusion.4
  (202 shorter events, 18.7 us)
Async XLA Ops:
  6.5 39.4 %reduce-scatter.7.cloned.1.call-start = ((), (), s32[]{:S(2)}) async-start(), calls=%async_computation.3 | async-start | bytes 327680 | tf_op jit(solution)/shard_map/reduce_scatter | solution.py:49
  7.3 6.6 %copy-start.3 = (f32[3200]{0:T(1024)S(1)}, f32[3200]{0:T(1024)}, u32[]{:S(2)}) copy-start(f32[3200]{0:T(1024)} %param.13) | copy-start | bytes 38404
  13.0 1.9 copy-start
  19.0 438.1 %reduce-scatter.5.cloned.1.call-start = ((), (), s32[]{:S(2)}) async-start(), calls=%async_computation.2 | async-start | bytes 7372800 | tf_op jit(solution)/shard_map/reduce_scatter | solution.py:87
  118.8 65.1 %copy-start.1 = (f32[32,512]{1,0:T(8,128)}, f32[32,512]{1,0:T(8,128)S(1)}, u32[]{:S(2)}) copy-start(f32[32,512]{1,0:T(8,128)S(1)} %pad.142) | copy-start | bytes 196612
  119.6 64.3 %copy-start.2 = (f32[32,512]{1,0:T(8,128)}, f32[32,512]{1,0:T(8,128)S(1)}, u32[]{:S(2)}) copy-start(f32[32,512]{1,0:T(8,128)S(1)} %pad.143) | copy-start | bytes 196612
Sparse Core Ops, SparseCore 0:
  19.1 26.7 reduce-scatter.6
  387.6 69.4 reduce-scatter.4
where the time goes:
time: 472 us; the launch traced here: 466 us
  blocking collectives  291 us (62%)
  waiting for transfers between devices  92.3 us (20%)
  local copies, waits for them, and re-layouts  46.5 us (10%)
  between operations  14 us (3%)
  other arithmetic  11.4 us (2%)
  matrix products  10.3 us (2%)
    all_gather x4, blocking collectives, prefix(): gathered = jax.tree.map(lambda a: lax.all_gather(a, axis), part)  283 us
    reduce_scatter x1, waiting for transfers between devices, per_device(): lax.psum_scatter(lax.dot_general(picked, residual, (((0,), (0,)), ((), ()...  65.4 us
    reduce_scatter x1, waiting for transfers between devices, per_device(): lax.psum_scatter(lax.dot_general(picked, weighted, (((1,), (1,)), ((), ()...  26.9 us
    dynamic_slice x31, local copies, waits for them, and re-layouts, one(): lax.dynamic_index_in_dim(a, source, 0, False)  23.1 us
    unnamed x16, local copies, waits for them, and re-layouts  12.7 us
  transfers between devices with their start and end apart: 2, of which 2 were waited for; matrix products, arithmetic and copies ran while one was open for 1% of the time, Pallas kernels for 0%

commit v1 on v0

v1 whole, which is shorter than its diff:
```python
import functools
import math

import jax
import jax.numpy as jnp
from jax import lax
from jax.experimental import pallas as pl
from jax.experimental.pallas import tpu as pltpu
from jax.sharding import PartitionSpec as P

LATENT_GROUP = 128
REGION = 128
CORES = 2
SUB = 8
F32 = jnp.float32
BF16 = jnp.bfloat16


def one_minus_exp_neg(x):
    series = jnp.full_like(x, 1.0 / 10.0)
    for n in range(9, 0, -1):
        series = (1.0 - x * series) * (1.0 / n)
    return jnp.where(x < 0.5, x * series, 1.0 - jnp.exp(-x))


def kernel(
    NT,
    NN,
    obs_ref,
    load_ref,
    mask_ref,
    prec_ref,
    rate_ref,
    lag_ref,
    out_ref,
    obs_all,
    weight,
    acc,
    drv_out,
    drv_in,
    dec_s,
    ret_s,
    x_s,
    parts,
    summ,
    enter_s,
    follow_s,
    sm_all,
    sm_t,
    out_s,
    obs_ss,
    obs_rs,
    drv_ss,
    drv_rs,
    summ_ss,
    summ_rs,
    sa_ss,
    sb_ss,
    sc_ss,
    sm_rs,
    out_ss,
    out_rs,
):
    frames, neurons = obs_ref.shape
    latents = load_ref.shape[0]
    groups, regions = mask_ref.shape
    LN = latents // NN
    LO = latents // NT
    NZ = NT // CORES
    steps = frames // SUB
    smin, smax = regions // NT, -(-regions // NT)
    me = lax.axis_index("tm")
    j = lax.axis_index("neuron")
    z, core = me // CORES, lax.rem(me, CORES)
    partner = z * CORES + 1 - core

    def first(o):
        return (o * regions + NT - 1) // NT

    def count(o):
        return first(o + 1) - first(o)

    def tm_at(d):
        return lax.rem(me + d, NT)

    def nn_at(d):
        return lax.rem(j + d, NN)

    def cols(r):
        return pl.ds(pl.multiple_of(r * REGION, REGION), REGION)

    def rows(b, n):
        return pl.ds(pl.multiple_of(b * n, n), n)

    def remote(src, dst, ss, rs, tm=None, nn=None):
        return pltpu.make_async_remote_copy(
            src_ref=src,
            dst_ref=dst,
            send_sem=ss,
            recv_sem=rs,
            device_id={"tm": me if tm is None else tm, "neuron": j if nn is None else nn},
            device_id_type=pl.DeviceIdType.MESH,
        )

    def guarded(s, owner, body):
        if s < smin:
            body()
        else:
            pl.when(s < count(owner))(body)

    barrier = pltpu.get_barrier_semaphore()
    for d in range(1, NT):
        pl.semaphore_signal(
            barrier, inc=1, device_id={"tm": tm_at(d), "neuron": j},
            device_id_type=pl.DeviceIdType.MESH,
        )
    for d in range(1, NN):
        pl.semaphore_signal(
            barrier, inc=1, device_id={"tm": me, "neuron": nn_at(d)},
            device_id_type=pl.DeviceIdType.MESH,
        )
    pl.semaphore_wait(barrier, NT + NN - 2)

    def obs_copy(s, d):
        o = tm_at(d)
        return remote(
            obs_ref.at[:, cols(first(o) + s)],
            obs_all.at[s, rows(me, frames), :],
            obs_ss.at[d, s],
            obs_rs.at[me, s],
            tm=o,
        )

    for s in range(smax):
        for d in range(1, NT):
            guarded(s, tm_at(d), lambda: obs_copy(s, d).start())

    per = 5 if regions % 5 == 0 else 1
    acc[...] = jnp.zeros_like(acc)

    def mask_value(g, r):
        return mask_ref[g, r].astype(F32)

    def effective(g, r):
        block = load_ref[pl.ds(g * LATENT_GROUP, LATENT_GROUP), cols(r)].astype(F32)
        return block * mask_value(g, r)

    @pl.loop(0, regions // per)
    def _(c):
        for q in range(per):
            r = c * per + q
            p_row = prec_ref[:, cols(r)]
            for g in range(groups):
                weight[pl.ds(g * LATENT_GROUP, LATENT_GROUP), pl.ds(q * REGION, REGION)] = (
                    effective(g, r) * p_row
                ).astype(BF16)
        width = per * REGION
        acc[...] += lax.dot_general(
            obs_ref[:, pl.ds(pl.multiple_of(c * width, width), width)],
            weight[...],
            (((1,), (1,)), ((), ())),
            preferred_element_type=F32,
        )

    def drv_copy(d):
        g = nn_at(d)
        return remote(
            drv_out.at[g], drv_in.at[j], drv_ss.at[d], drv_rs.at[j], nn=g
        )

    for g in range(NN):
        drv_out[g] = acc[:, g * LN : (g + 1) * LN]
    for d in range(1, NN):
        drv_copy(d).start()
    drv_in[j] = drv_out[j]

    rate = jnp.zeros((frames, LN), F32)
    lag = jnp.zeros((1, LN), F32)
    for g in range(NN):
        mine = j == g
        rate = jnp.where(mine, rate_ref[:, g * LN : (g + 1) * LN].astype(F32), rate)
        lag = jnp.where(mine, lag_ref[:, g * LN : (g + 1) * LN], lag)
    dec_s[...] = jnp.exp(-rate)
    ret_s[...] = jnp.exp(-(rate * lag))
    innovation = jnp.sqrt(one_minus_exp_neg(2.0 * rate))

    for d in range(1, NN):
        g = nn_at(d)
        remote(drv_out.at[g], drv_in.at[g], drv_ss.at[d], drv_rs.at[g], nn=g).wait_recv()
    total = drv_in[0]
    for g in range(1, NN):
        total = total + drv_in[g]
    x_s[...] = innovation * total

    def at(ref, i):
        return ref[pl.ds(i, SUB, stride=steps), :]

    mult = jnp.ones((SUB, LN), F32)
    add = jnp.zeros((SUB, LN), F32)
    fwd = []
    for i in range(steps):
        dec = at(dec_s, i)
        mult = dec * mult
        add = dec * add + at(x_s, i)
        fwd.append((mult, add))
    pm, pa = [jnp.ones((1, LN), F32)], [jnp.zeros((1, LN), F32)]
    for s in range(SUB):
        pm.append(mult[s : s + 1] * pm[-1])
        pa.append(mult[s : s + 1] * pa[-1] + add[s : s + 1])
    pm_all = jnp.concatenate(pm[:SUB], axis=0)
    pa_all = jnp.concatenate(pa[:SUB], axis=0)
    rm = jnp.ones((SUB, LN), F32)
    sv = jnp.zeros((SUB, LN), F32)
    uv = jnp.zeros((SUB, LN), F32)
    bwd = [None] * steps
    for i in reversed(range(steps)):
        ret = at(ret_s, i)
        m_i, a_i = fwd[i]
        keep = 1.0 - ret
        rm = ret * rm
        sv = ret * sv + keep * (a_i + m_i * pa_all)
        uv = ret * uv + keep * (m_i * pm_all)
        bwd[i] = (rm, sv, uv)
    rr, ss, uu = (
        [jnp.ones((1, LN), F32)],
        [jnp.zeros((1, LN), F32)],
        [jnp.zeros((1, LN), F32)],
    )
    for s in reversed(range(SUB)):
        r_s = rm[s : s + 1]
        rr.append(r_s * rr[-1])
        ss.append(r_s * ss[-1] + sv[s : s + 1])
        uu.append(r_s * uu[-1] + uv[s : s + 1])
    rr_all = jnp.concatenate(rr[:SUB][::-1], axis=0)
    ss_all = jnp.concatenate(ss[:SUB][::-1], axis=0)
    uu_all = jnp.concatenate(uu[:SUB][::-1], axis=0)
    zero = jnp.zeros((1, LN), F32)
    summ[me] = jnp.concatenate(
        [pm[SUB], pa[SUB], rr[SUB], ss[SUB], uu[SUB], zero, zero, zero], axis=0
    )

    def summ_copy(d):
        o = tm_at(d)
        return remote(summ.at[me], summ.at[me], summ_ss.at[d], summ_rs.at[me], tm=o)

    for d in range(1, NT):
        summ_copy(d).start()
    for i in range(steps):
        rm_i, s_i, u_i = bwd[i]
        parts[0, i] = s_i + rm_i * ss_all
        parts[1, i] = u_i + rm_i * uu_all
        parts[2, i] = rm_i * rr_all
    for d in range(1, NT):
        o = tm_at(d)
        remote(summ.at[o], summ.at[o], summ_ss.at[d], summ_rs.at[o], tm=o).wait_recv()

    entering = [zero]
    for b in range(NT):
        enter_s[b] = jnp.broadcast_to(entering[b], (SUB, LN))
        entering.append(summ[b, 0:1] * entering[b] + summ[b, 1:2])
    following = zero
    for b in reversed(range(NT)):
        follow_s[b] = jnp.broadcast_to(following, (SUB, LN))
        following = summ[b, 2:3] * following + summ[b, 3:4] + summ[b, 4:5] * entering[b]
    e_me, f_me = enter_s[me], follow_s[me]
    for i in range(steps):
        x_s[pl.ds(i, SUB, stride=steps), :] = parts[0, i] + parts[1, i] * e_me + parts[2, i] * f_me
    sm_all[j, rows(me, frames), :] = x_s[...].astype(BF16)

    def block(g, b):
        return sm_all.at[g, rows(b, frames), :]

    def z_at(d):
        return lax.rem(z + d, NZ) * CORES + core

    def send_z(d):
        return remote(block(j, me), block(j, me), sa_ss.at[d], sm_rs.at[me, j], tm=z_at(d))

    def send_n(dz, d):
        b = z_at(dz)
        return remote(block(j, b), block(j, b), sb_ss.at[dz, d], sm_rs.at[b, j], nn=nn_at(d))

    def send_c(dz, d):
        b, g = z_at(dz), nn_at(d)
        return remote(block(g, b), block(g, b), sc_ss.at[dz, d], sm_rs.at[b, g], tm=partner)

    def arrive(b, g):
        remote(block(g, b), block(g, b), sa_ss.at[0], sm_rs.at[b, g], tm=partner).wait_recv()

    def turn(b, g):
        sm_t[g, :, rows(b, frames)] = sm_all[g, rows(b, frames), :].T

    for d in range(1, NZ):
        send_z(d).start()
    for dz in range(NZ):
        if dz > 0:
            arrive(z_at(dz), j)
        for d in range(1, NN):
            send_n(dz, d).start()
        send_c(dz, 0).start()
    for dz in range(NZ):
        turn(z_at(dz), j)
    for dz in range(NZ):
        for d in range(1, NN):
            g = nn_at(d)
            arrive(z_at(dz), g)
            send_c(dz, d).start()
            turn(z_at(dz), g)
    for dz in range(NZ):
        for d in range(NN):
            b = lax.rem(z + dz, NZ) * CORES + 1 - core
            arrive(b, nn_at(d))
            turn(b, nn_at(d))

    scale = 1.0 / math.sqrt(frames * NT)
    obs_all_own = []
    for s in range(smax):
        guarded(
            s,
            me,
            lambda: obs_all.__setitem__(
                (s, rows(me, frames), slice(None)), obs_ref[:, cols(first(me) + s)]
            ),
        )

    def out_copy(s, d):
        o = tm_at(d)
        return remote(
            out_s.at[s, rows(o, LO), :],
            out_ref.at[:, cols(first(me) + s)],
            out_ss.at[d, s],
            out_rs.at[me, s],
            tm=o,
        )

    def slot(s):
        r = first(me) + s
        for d in range(1, NT):
            o = tm_at(d)
            there = obs_all.at[s, rows(o, frames), :]
            remote(there, there, obs_ss.at[d, s], obs_rs.at[o, s], tm=o).wait_recv()
        eff = jnp.concatenate([effective(g, r) for g in range(groups)], axis=0).astype(BF16)
        smooth = jnp.concatenate([sm_all[g] for g in range(NN)], axis=1)
        rebuilt = jnp.dot(smooth, eff, preferred_element_type=F32)
        residual = ((obs_all[s].astype(F32) - rebuilt) * prec_ref[:, cols(r)]).astype(BF16)
        smooth_t = sm_t[...].reshape(latents, NT * frames)
        summed = jnp.dot(smooth_t, residual, preferred_element_type=F32) * scale
        for g in range(groups):
            out_s[s, pl.ds(g * LATENT_GROUP, LATENT_GROUP), :] = (
                summed[g * LATENT_GROUP : (g + 1) * LATENT_GROUP] * mask_value(g, r)
            ).astype(BF16)
        for d in range(1, NT):
            out_copy(s, d).start()
        out_ref[:, cols(r)] = out_s[s, rows(me, LO), :]

    for s in range(smax):
        guarded(s, me, lambda: slot(s))

    for s in range(smax):
        for d in range(1, NT):
            o = tm_at(d)

            def landed():
                there = out_ref.at[:, cols(first(o) + s)]
                remote(there, there, out_ss.at[d, s], out_rs.at[o, s], tm=o).wait_recv()

            guarded(s, o, landed)

    for d in range(1, NT):
        summ_copy(d).wait_send()
        for s in range(smax):
            guarded(s, tm_at(d), lambda: obs_copy(s, d).wait_send())
            guarded(s, me, lambda: out_copy(s, d).wait_send())
    for d in range(1, NN):
        drv_copy(d).wait_send()
    for d in range(1, NZ):
        send_z(d).wait_send()
    for dz in range(NZ):
        for d in range(1, NN):
            send_n(dz, d).wait_send()
        for d in range(NN):
            send_c(dz, d).wait_send()


def per_device(NT, NN, observations, loadings, region_mask, precision, decay_rate, smoothing_lag):
    frames, neurons = observations.shape
    latents = loadings.shape[0]
    regions = region_mask.shape[1]
    LN, LO, NZ = latents // NN, latents // NT, NT // CORES
    smax = -(-regions // NT)
    steps = frames // SUB
    per = 5 if regions % 5 == 0 else 1
    dma = pltpu.SemaphoreType.DMA
    vm = pl.BlockSpec(memory_space=pltpu.VMEM)
    return pl.pallas_call(
        functools.partial(kernel, NT, NN),
        out_shape=jax.ShapeDtypeStruct((LO, neurons), BF16),
        in_specs=[vm, vm, pl.BlockSpec(memory_space=pltpu.SMEM), vm, vm, vm],
        out_specs=vm,
        scratch_shapes=[
            pltpu.VMEM((smax, NT * frames, REGION), BF16),
            pltpu.VMEM((latents, per * REGION), BF16),
            pltpu.VMEM((frames, latents), F32),
            pltpu.VMEM((NN, frames, LN), F32),
            pltpu.VMEM((NN, frames, LN), F32),
            pltpu.VMEM((frames, LN), F32),
            pltpu.VMEM((frames, LN), F32),
            pltpu.VMEM((frames, LN), F32),
            pltpu.VMEM((3, steps, SUB, LN), F32),
            pltpu.VMEM((NT, SUB, LN), F32),
            pltpu.VMEM((NT, SUB, LN), F32),
            pltpu.VMEM((NT, SUB, LN), F32),
            pltpu.VMEM((NN, NT * frames, LN), BF16),
            pltpu.VMEM((NN, LN, NT * frames), BF16),
            pltpu.VMEM((smax, latents, REGION), BF16),
            dma((NT, smax)),
            dma((NT, smax)),
            dma((NN,)),
            dma((NN,)),
            dma((NT,)),
            dma((NT,)),
            dma((NZ,)),
            dma((NZ, NN)),
            dma((NZ, NN)),
            dma((NT, NN)),
            dma((NT, smax)),
            dma((NT, smax)),
        ],
        compiler_params=pltpu.CompilerParams(
            collective_id=0, has_side_effects=True, vmem_limit_bytes=48 * 1024 * 1024
        ),
    )(
        observations,
        loadings,
        region_mask,
        precision.reshape(1, neurons),
        decay_rate,
        smoothing_lag.reshape(1, latents),
    )


def solution(mesh):
    return jax.shard_map(
        functools.partial(per_device, mesh.shape["tm"], mesh.shape["neuron"]),
        mesh=mesh,
        in_specs=(
            P("tm", "neuron"),
            P(None, "neuron"),
            P(None, "neuron"),
            P("neuron"),
            P("tm", None),
            P(),
        ),
        out_specs=P("tm", "neuron"),
        check_vma=False,
    )
```

time: 472 us -> 57.4 us (0.12); the launches traced: 466 us -> 57.1 us
  blocking collectives: 291 us -> 0 us
  waiting for transfers between devices: 92.3 us -> 0 us
  Pallas kernels: 0 us -> 50.3 us
  local copies, waits for them, and re-layouts: 46.5 us -> 6.81 us
  between operations: 14 us -> 0.02 us
  other arithmetic: 11.4 us -> 0 us
  matrix products: 10.3 us -> 0 us
    all_gather x5 -> x0, blocking collectives: 291 us -> none  [the longest x4 283 us: prefix(): gathered = jax.tree.map(lambda a: lax.all_gather(a, axis), part)]
    reduce_scatter x2 -> x0, waiting for transfers between devices: 92.3 us -> none  [the longest x1 65.4 us: per_device(): lax.psum_scatter(lax.dot_general(picked, residual, (((0,), (0,)), ((), ()...]
    pallas_call x0 -> x1, Pallas kernels: none -> 50.3 us  [per_device(): pl.pallas_call(functools.partial(kernel, NT, NN), out_shape=jax.ShapeDtyp...]
    dynamic_slice x32 -> x0, local copies, waits for them, and re-layouts: 24.8 us -> none  [the longest x31 23.1 us: one(): lax.dynamic_index_in_dim(a, source, 0, False)]
    dot_general x2 -> x0, matrix products: 10.3 us -> none  [the longest x1 7.04 us: per_device(): lax.dot_general(picked, residual, (((0,), (0,)), ((), ())), preferred_ele...]
    unnamed x16 -> x11, local copies, waits for them, and re-layouts: 12.7 us -> 6.09 us
  transfers between devices with their start and end apart: 2 -> 0, of which waited for: 2 -> 0; matrix products, arithmetic and copies ran while one was open for 1% -> 0% of each run, Pallas kernels for 0% -> 0%
where the time goes in v1:
time: 57.4 us; the launch traced here: 57.1 us
  Pallas kernels  50.3 us (88%)
  local copies, waits for them, and re-layouts  6.81 us (12%)
    pallas_call x1, Pallas kernels, per_device(): pl.pallas_call(functools.partial(kernel, NT, NN), out_shape=jax.ShapeDtyp...  50.3 us
    unnamed x11, local copies, waits for them, and re-layouts  6.09 us

profile of v1, /device:TPU:0, one launch (start us, length us, event | category | flops | bytes accessed | tf_op | source)
XLA Modules:
  0.0 57.1 jit_solution(16548426633797929259)
XLA Ops:
  0.0 0.7 %reshape.6.prec_ref = f32[1,3200]{1,0:T(1,128)S(1)} reshape(f32[3200]{0:T(1024)} %param.9) | data formatting | bytes 25600 | tf_op jit(solution)/shard_map/reshape | solution.py:436
  0.7 0.0 copy-start
  0.7 1.9 %copy-done = bf16[512,3200]{1,0:T(8,128)(2,1)S(1)} copy-done((bf16[512,3200]{1,0:T(8,128)(2,1)S(1)}, bf16[512,3200]{1,0:T(8,128)(2,1)}, u32[]{:S(2)}) %copy-start) | copy-done | bytes 3276824
  2.7 0.0 copy-start.1
  2.7 1.1 %copy-done.1 = bf16[128,3200]{1,0:T(8,128)(2,1)S(1)} copy-done((bf16[128,3200]{1,0:T(8,128)(2,1)S(1)}, bf16[128,3200]{1,0:T(8,128)(2,1)}, u32[]{:S(2)}) %copy-start.1) | copy-done | bytes 819224
  3.8 0.0 copy-start.2
  3.8 0.9 %copy-done.2 = bf16[128,512]{1,0:T(8,128)(2,1)S(1)} copy-done((bf16[128,512]{1,0:T(8,128)(2,1)S(1)}, bf16[128,512]{1,0:T(8,128)(2,1)}, u32[]{:S(2)}) %copy-start.2) | copy-done | bytes 131096
  4.7 0.0 copy-start.3
  4.7 0.7 %copy-done.3 = s32[4,25]{1,0:T(4,128)S(1)} copy-done((s32[4,25]{1,0:T(4,128)S(1)}, s32[4,25]{1,0:T(4,128)}, u32[]{:S(2)}) %copy-start.3) | copy-done | bytes 424
  5.4 0.0 copy-start.4
  5.4 0.7 %copy-done.4 = f32[512]{0:T(512)S(1)} copy-done((f32[512]{0:T(512)S(1)}, f32[512]{0:T(512)}, u32[]{:S(2)}) %copy-start.4) | copy-done | bytes 2072
  6.1 50.3 %shard_map.64 = bf16[64,3200]{1,0:T(8,128)(2,1)S(1)} custom-call(bf16[128,3200]{1,0:T(8,128)(2,1)S(1)} %copy-done.1, bf16[512,3200]{1,0:T(8,128)(2,1)S(1)} %copy-done, s32[4,25]{1,0:T(4,128)S(1)} %copy-done.3, f32[1,3200]{1,0:T(1,128)S(1)} %reshape.6.prec_ref, bf16[128,512]{1,0:T(8,128)(2,1)S(1)} %copy-done.2, f32[1,512]{1,0:T(1,128)S(1)} %bitcast.1), custom_call_target="tpu_custom_call" | custom-call | tf_op jit(solution)/shard_map/pallas_call | solution.py:395
  56.4 0.8 %copy.8 = bf16[64,3200]{1,0:T(8,128)(2,1)} copy(bf16[64,3200]{1,0:T(8,128)(2,1)S(1)} %shard_map.64) | data formatting | bytes 819200
Async XLA Ops:
  0.7 1.9 %copy-start = (bf16[512,3200]{1,0:T(8,128)(2,1)S(1)}, bf16[512,3200]{1,0:T(8,128)(2,1)}, u32[]{:S(2)}) copy-start(bf16[512,3200]{1,0:T(8,128)(2,1)} %load_ref.1) | copy-start | bytes 9830404
  2.7 1.1 %copy-start.1 = (bf16[128,3200]{1,0:T(8,128)(2,1)S(1)}, bf16[128,3200]{1,0:T(8,128)(2,1)}, u32[]{:S(2)}) copy-start(bf16[128,3200]{1,0:T(8,128)(2,1)} %obs_ref.1) | copy-start | bytes 2457604
  3.8 0.9 %copy-start.2 = (bf16[128,512]{1,0:T(8,128)(2,1)S(1)}, bf16[128,512]{1,0:T(8,128)(2,1)}, u32[]{:S(2)}) copy-start(bf16[128,512]{1,0:T(8,128)(2,1)} %rate_ref.1) | copy-start | bytes 393220
  4.7 0.7 %copy-start.3 = (s32[4,25]{1,0:T(4,128)S(1)}, s32[4,25]{1,0:T(4,128)}, u32[]{:S(2)}) copy-start(s32[4,25]{1,0:T(4,128)} %mask_ref.1) | copy-start | bytes 1204
  5.4 0.7 %copy-start.4 = (f32[512]{0:T(512)S(1)}, f32[512]{0:T(512)}, u32[]{:S(2)}) copy-start(f32[512]{0:T(512)} %param.11) | copy-start | bytes 6148

commit v2 on v1

--- a/solution.py
+++ b/solution.py
@@ -11,6 +11,7 @@
 LATENT_GROUP = 128
 REGION = 128
 CORES = 2
+EARLY = 2
 SUB = 8
 F32 = jnp.float32
 BF16 = jnp.bfloat16
@@ -26,13 +27,21 @@
 def kernel(
     NT,
     NN,
+    obs_hbm,
+    load_hbm,
+    mask_hbm,
+    prec_hbm,
+    rate_hbm,
+    lag_hbm,
+    out_ref,
     obs_ref,
     load_ref,
     mask_ref,
     prec_ref,
     rate_ref,
     lag_ref,
-    out_ref,
+    in_sem,
+    load_sem,
     obs_all,
     weight,
     acc,
@@ -80,11 +89,21 @@
     def count(o):
         return first(o + 1) - first(o)
 
+    def peer(i, d, n):
+        if n & (n - 1):
+            return lax.rem(i + d, n)
+        bit = 1
+        while bit < n:
+            if d & bit:
+                i = i + bit - 2 * bit * lax.rem(i // bit, 2)
+            bit *= 2
+        return i
+
     def tm_at(d):
-        return lax.rem(me + d, NT)
+        return peer(me, d, NT)
 
     def nn_at(d):
-        return lax.rem(j + d, NN)
+        return peer(j, d, NN)
 
     def cols(r):
         return pl.ds(pl.multiple_of(r * REGION, REGION), REGION)
@@ -108,6 +127,32 @@
         else:
             pl.when(s < count(owner))(body)
 
+    per = 5 if regions % 5 == 0 else 1
+    width = per * REGION
+
+    def load_copy(c):
+        where = pl.ds(pl.multiple_of(c * width, width), width)
+        return pltpu.make_async_copy(load_hbm.at[:, where], load_ref.at[:, where], load_sem.at[c])
+
+    inputs = [
+        pltpu.make_async_copy(a, b, in_sem.at[i])
+        for i, (a, b) in enumerate(
+            [
+                (mask_hbm, mask_ref),
+                (prec_hbm, prec_ref),
+                (obs_hbm, obs_ref),
+                (rate_hbm, rate_ref),
+                (lag_hbm, lag_ref),
+            ]
+        )
+    ]
+    for copy in inputs[:3]:
+        copy.start()
+    for c in range(regions // per):
+        load_copy(c).start()
+    for copy in inputs[3:]:
+        copy.start()
+
     barrier = pltpu.get_barrier_semaphore()
     for d in range(1, NT):
         pl.semaphore_signal(
@@ -124,18 +169,23 @@
     def obs_copy(s, d):
         o = tm_at(d)
         return remote(
-            obs_ref.at[:, cols(first(o) + s)],
+            obs_hbm.at[:, cols(first(o) + s)],
             obs_all.at[s, rows(me, frames), :],
             obs_ss.at[d, s],
             obs_rs.at[me, s],
             tm=o,
         )
 
-    for s in range(smax):
-        for d in range(1, NT):
-            guarded(s, tm_at(d), lambda: obs_copy(s, d).start())
-
-    per = 5 if regions % 5 == 0 else 1
+    def send_obs(slots):
+        for s in slots:
+            for d in range(1, NT):
+                guarded(s, tm_at(d), lambda: obs_copy(s, d).start())
+
+    early = min(EARLY, smax)
+    send_obs(range(early))
+
+    for copy in inputs[:3]:
+        copy.wait()
     acc[...] = jnp.zeros_like(acc)
 
     def mask_value(g, r):
@@ -147,14 +197,14 @@
 
     @pl.loop(0, regions // per)
     def _(c):
+        load_copy(c).wait()
         for q in range(per):
             r = c * per + q
-            p_row = prec_ref[:, cols(r)]
+            p_row = prec_ref[pl.ds(r, 1), :]
             for g in range(groups):
                 weight[pl.ds(g * LATENT_GROUP, LATENT_GROUP), pl.ds(q * REGION, REGION)] = (
                     effective(g, r) * p_row
                 ).astype(BF16)
-        width = per * REGION
         acc[...] += lax.dot_general(
             obs_ref[:, pl.ds(pl.multiple_of(c * width, width), width)],
             weight[...],
@@ -169,15 +219,17 @@
         )
 
     for g in range(NN):
-        drv_out[g] = acc[:, g * LN : (g + 1) * LN]
+        drv_out[g] = acc[:, g * LN : (g + 1) * LN].astype(BF16)
     for d in range(1, NN):
         drv_copy(d).start()
-    drv_in[j] = drv_out[j]
-
+    for copy in inputs[3:]:
+        copy.wait()
+    own = jnp.zeros((frames, LN), F32)
     rate = jnp.zeros((frames, LN), F32)
     lag = jnp.zeros((1, LN), F32)
     for g in range(NN):
         mine = j == g
+        own = jnp.where(mine, acc[:, g * LN : (g + 1) * LN], own)
         rate = jnp.where(mine, rate_ref[:, g * LN : (g + 1) * LN].astype(F32), rate)
         lag = jnp.where(mine, lag_ref[:, g * LN : (g + 1) * LN], lag)
     dec_s[...] = jnp.exp(-rate)
@@ -187,9 +239,9 @@
     for d in range(1, NN):
         g = nn_at(d)
         remote(drv_out.at[g], drv_in.at[g], drv_ss.at[d], drv_rs.at[g], nn=g).wait_recv()
-    total = drv_in[0]
-    for g in range(1, NN):
-        total = total + drv_in[g]
+    total = own
+    for d in range(1, NN):
+        total = total + drv_in[nn_at(d)].astype(F32)
     x_s[...] = innovation * total
 
     def at(ref, i):
@@ -271,7 +323,7 @@
         return sm_all.at[g, rows(b, frames), :]
 
     def z_at(d):
-        return lax.rem(z + d, NZ) * CORES + core
+        return peer(z, d, NZ) * CORES + core
 
     def send_z(d):
         return remote(block(j, me), block(j, me), sa_ss.at[d], sm_rs.at[me, j], tm=z_at(d))
@@ -292,13 +344,13 @@
 
     for d in range(1, NZ):
         send_z(d).start()
+    send_obs(range(early, smax))
     for dz in range(NZ):
         if dz > 0:
             arrive(z_at(dz), j)
         for d in range(1, NN):
             send_n(dz, d).start()
         send_c(dz, 0).start()
-    for dz in range(NZ):
         turn(z_at(dz), j)
     for dz in range(NZ):
         for d in range(1, NN):
@@ -308,12 +360,11 @@
             turn(z_at(dz), g)
     for dz in range(NZ):
         for d in range(NN):
-            b = lax.rem(z + dz, NZ) * CORES + 1 - core
+            b = peer(z, dz, NZ) * CORES + 1 - core
             arrive(b, nn_at(d))
             turn(b, nn_at(d))
 
     scale = 1.0 / math.sqrt(frames * NT)
-    obs_all_own = []
     for s in range(smax):
         guarded(
             s,
@@ -342,7 +393,7 @@
         eff = jnp.concatenate([effective(g, r) for g in range(groups)], axis=0).astype(BF16)
         smooth = jnp.concatenate([sm_all[g] for g in range(NN)], axis=1)
         rebuilt = jnp.dot(smooth, eff, preferred_element_type=F32)
-        residual = ((obs_all[s].astype(F32) - rebuilt) * prec_ref[:, cols(r)]).astype(BF16)
+        residual = ((obs_all[s].astype(F32) - rebuilt) * prec_ref[pl.ds(r, 1), :]).astype(BF16)
         smooth_t = sm_t[...].reshape(latents, NT * frames)
         summed = jnp.dot(smooth_t, residual, preferred_element_type=F32) * scale
         for g in range(groups):
@@ -391,18 +442,26 @@
     steps = frames // SUB
     per = 5 if regions % 5 == 0 else 1
     dma = pltpu.SemaphoreType.DMA
-    vm = pl.BlockSpec(memory_space=pltpu.VMEM)
+    hbm = pl.BlockSpec(memory_space=pltpu.HBM)
     return pl.pallas_call(
         functools.partial(kernel, NT, NN),
         out_shape=jax.ShapeDtypeStruct((LO, neurons), BF16),
-        in_specs=[vm, vm, pl.BlockSpec(memory_space=pltpu.SMEM), vm, vm, vm],
-        out_specs=vm,
+        in_specs=[hbm] * 6,
+        out_specs=pl.BlockSpec(memory_space=pltpu.VMEM),
         scratch_shapes=[
+            pltpu.VMEM((frames, neurons), BF16),
+            pltpu.VMEM((latents, neurons), BF16),
+            pltpu.SMEM(region_mask.shape, jnp.int32),
+            pltpu.VMEM((regions, REGION), F32),
+            pltpu.VMEM((frames, latents), BF16),
+            pltpu.VMEM((1, latents), F32),
+            dma((5,)),
+            dma((regions // per,)),
             pltpu.VMEM((smax, NT * frames, REGION), BF16),
             pltpu.VMEM((latents, per * REGION), BF16),
             pltpu.VMEM((frames, latents), F32),
-            pltpu.VMEM((NN, frames, LN), F32),
-            pltpu.VMEM((NN, frames, LN), F32),
+            pltpu.VMEM((NN, frames, LN), BF16),
+            pltpu.VMEM((NN, frames, LN), BF16),
             pltpu.VMEM((frames, LN), F32),
             pltpu.VMEM((frames, LN), F32),
             pltpu.VMEM((frames, LN), F32),
@@ -427,13 +486,13 @@
             dma((NT, smax)),
         ],
         compiler_params=pltpu.CompilerParams(
-            collective_id=0, has_side_effects=True, vmem_limit_bytes=48 * 1024 * 1024
+            collective_id=0, has_side_effects=True, vmem_limit_bytes=63 * 1024 * 1024
         ),
     )(
         observations,
         loadings,
         region_mask,
-        precision.reshape(1, neurons),
+        precision.reshape(regions, REGION),
         decay_rate,
         smoothing_lag.reshape(1, latents),
     )

time: 57.4 us -> 46.4 us (0.81)
  Pallas kernels: 50.3 us -> 44.5 us
  local copies, waits for them, and re-layouts: 6.81 us -> 1.78 us
    pallas_call x1, Pallas kernels: 50.3 us -> 44.5 us  [per_device(): pl.pallas_call(functools.partial(kernel, NT, NN), out_shape=jax.ShapeDtyp...]
    unnamed x11 -> x1, local copies, waits for them, and re-layouts: 6.09 us -> 1.78 us
    reshape x1 -> x0, local copies, waits for them, and re-layouts: 0.73 us -> none  [per_device(): precision.reshape(1, neurons)]
where the time goes in v2:
time: 46.4 us; the launch traced here: 46.3 us
  Pallas kernels  44.5 us (96%)
  local copies, waits for them, and re-layouts  1.78 us (4%)
    pallas_call x1, Pallas kernels, per_device(): pl.pallas_call(functools.partial(kernel, NT, NN), out_shape=jax.ShapeDtyp...  44.5 us
    unnamed x1, local copies, waits for them, and re-layouts  1.78 us

profile of v2, /device:TPU:0, one launch (start us, length us, event | category | flops | bytes accessed | tf_op | source)
XLA Modules:
  0.0 46.3 jit_solution(7307051116906128670)
XLA Ops:
  0.0 44.5 %shard_map.64 = bf16[64,3200]{1,0:T(8,128)(2,1)} custom-call(bf16[128,3200]{1,0:T(8,128)(2,1)} %obs_hbm.1, bf16[512,3200]{1,0:T(8,128)(2,1)} %load_hbm.1, s32[4,25]{1,0:T(4,128)} %mask_hbm.1, f32[25,128]{1,0:T(8,128)} %bitcast.2, bf16[128,512]{1,0:T(8,128)(2,1)} %rate_hbm.1, f32[1,512]{1,0:T(1,128)} %bitcast.3), custom_call_target="tpu_custom_call" | custom-call | tf_op jit(solution)/shard_map/pallas_call | solution.py:446
  44.5 1.8 %copy.8 = bf16[64,3200]{1,0:T(8,128)(2,1)} copy(bf16[64,3200]{1,0:T(8,128)(2,1)} %shard_map.64) | data formatting | bytes 819200
